TPU v7x, 128 devices: a whole 4x4x4 slice. The times are simulated.
128 devices in a mesh: seq: 64 (over x, y, z_lo, core), head: 2 (over z_hi).
Axes of the slice: x: 4, y: 4, z: 4 (z_hi: 2, z_lo: 2; z = z_hi * 2 + z_lo), core: 2. Of those that a mesh axis runs over, the one named last changes fastest.
Arguments:
- queries: bfloat16 [2, 32768, 1024], P(None, 'seq', 'head'), may hold values from -40 to 40, as said below
- keys: bfloat16 [2, 32768, 1024], P(None, 'seq', 'head'), may hold values from -40 to 40, as said below
- values: bfloat16 [2, 32768, 1024], P(None, 'seq', 'head'), may hold values from -6 to 6
- token_rate: float32 [2, 4, 32768], P(None, 'head', 'seq'), may hold values from 0.05 to 1
- step_size: float32 [4], P('head'), may hold values from 0.5 to 1
- w_gate: float32 [4, 512, 256], P('head'), may hold values from -0.375 to 0.375
- w_up: float32 [4, 512, 256], P('head'), may hold values from -0.375 to 0.375
- w_down: float32 [4, 256, 512], P('head'), may hold values from -0.25 to 0.25
- w_out: bfloat16 [1024, 1024], P('head'), may hold values from -0.1875 to 0.1875
Outputs:
- mixed: bfloat16 [2, 32768, 1024], P(None, 'seq', 'head')
- gate_state: float32 [4, 512, 256], P('head')
- up_state: float32 [4, 512, 256], P('head')
- down_state: float32 [4, 256, 512], P('head')
Inputs may be any that keep to these rules, and one draw needn't show every extreme that they name: `queries`: Real-valued entries. `keys`: Real-valued entries.
All inputs are finite; a program needn't handle non-finite values.
Results may differ from a plain program's by a relative error of at most 0.028.
Values may be sent and summed in bfloat16 or wider, within the bound.
A program may use at most 128 MiB of HBM per device.

v0:
```python
import math

import jax
import jax.numpy as jnp
from jax import lax
from jax.sharding import PartitionSpec as P

DH = 256
WIN = 256
NS_STEPS = 5
SEGMENTS = 2


coef_a = 3.4445
coef_b = -4.775
coef_c = 2.0315
tiny = 1e-07
highest = lax.Precision.HIGHEST


def shifted(value, axis, steps):
    count = lax.axis_size(axis)
    first, last = (max(0, -steps), min(count, count - steps))
    return lax.ppermute(value, axis, [(source, source + steps) for source in range(first, last)])


def window_attention(queries, keys, values, rim_keys, rim_values, position):
    seg_count, token_count, feat_width = queries.shape
    heads_here = feat_width // DH
    block_rows = min(512, token_count)
    key_all = jnp.concatenate([rim_keys, keys], axis=1).reshape(
        seg_count, WIN + token_count, heads_here, DH
    )
    value_all = jnp.concatenate([rim_values, values], axis=1).reshape(
        seg_count, WIN + token_count, heads_here, DH
    )
    query_heads = queries.reshape(seg_count, token_count, heads_here, DH)
    row_ids = lax.broadcasted_iota(jnp.int32, (block_rows, block_rows + WIN), 0)
    col_ids = lax.broadcasted_iota(jnp.int32, (block_rows, block_rows + WIN), 1)
    distance = row_ids + WIN - col_ids
    scores = jnp.einsum(
        "cqhd,ckhd->chqk", query_heads, key_all, preferred_element_type=jnp.float32
    ) / math.sqrt(DH)
    allowed = (distance >= 0) & (distance < WIN) & (position + 0 + col_ids - WIN >= 0)
    scores = jnp.where(allowed[None, None], scores, -1e30)
    row_max = jnp.max(scores, axis=-1, keepdims=True)
    weights = jnp.exp(scores - row_max)
    probs = (weights / jnp.sum(weights, axis=-1, keepdims=True)).astype(jnp.bfloat16)
    results = jnp.einsum("chqk,ckhd->cqhd", probs, value_all, preferred_element_type=jnp.float32)
    return results.reshape(seg_count, token_count, feat_width)


def segment_gradients(key_rows, value_rows, rate_rows, gate_copy, up_copy, down_copy):
    token_count = key_rows.shape[0]
    heads_here = gate_copy.shape[0]
    key_heads = key_rows.reshape(token_count, heads_here, DH)
    value_heads = jnp.swapaxes(value_rows.reshape(token_count, heads_here, DH), 0, 1)
    gate_pre = jnp.einsum("thd,hfd->htf", key_heads, gate_copy, preferred_element_type=jnp.float32)
    up_pre = jnp.einsum("thd,hfd->htf", key_heads, up_copy, preferred_element_type=jnp.float32)
    sigmoid_gate = jax.nn.sigmoid(gate_pre)
    gate_act = gate_pre * sigmoid_gate
    hidden_act = (gate_act * up_pre).astype(jnp.bfloat16)
    error_rows = (-(rate_rows[:, :, None] * value_heads)).astype(jnp.bfloat16)
    back_act = jnp.einsum("htd,hdf->htf", error_rows, down_copy, preferred_element_type=jnp.float32)
    grad_gate_pre = (
        back_act * up_pre * sigmoid_gate * (1.0 + gate_pre * (1.0 - sigmoid_gate))
    ).astype(jnp.bfloat16)
    grad_up_pre = (back_act * gate_act).astype(jnp.bfloat16)
    grad_gate = jnp.einsum(
        "htf,thd->hfd", grad_gate_pre, key_heads, preferred_element_type=jnp.float32
    )
    grad_up = jnp.einsum("htf,thd->hfd", grad_up_pre, key_heads, preferred_element_type=jnp.float32)
    grad_down = jnp.einsum(
        "htf,htd->hfd", hidden_act, error_rows, preferred_element_type=jnp.float32
    )
    return jnp.stack([grad_gate, grad_up, grad_down], axis=1)


def apply_fast(query_rows, gate_copy, up_copy, down_copy):
    token_count, feat_width = query_rows.shape
    heads_here = gate_copy.shape[0]
    query_heads = query_rows.reshape(token_count, heads_here, DH)
    gate_pre = jnp.einsum(
        "thd,hfd->htf", query_heads, gate_copy, preferred_element_type=jnp.float32
    )
    up_pre = jnp.einsum("thd,hfd->htf", query_heads, up_copy, preferred_element_type=jnp.float32)
    hidden_act = (jax.nn.silu(gate_pre) * up_pre).astype(jnp.bfloat16)
    fast_out = jnp.einsum("htf,hdf->thd", hidden_act, down_copy, preferred_element_type=jnp.float32)
    return fast_out.reshape(token_count, feat_width)


def gram_local(rows):
    return jnp.einsum("hmfd,hmfe->hmde", rows, rows, precision=highest)


def newton_schulz(rows, first_gram, gram_fn):
    current = rows
    gram = first_gram
    for step_index in range(NS_STEPS):
        if step_index > 0:
            gram = gram_fn(current)
        square = jnp.einsum("hmde,hmef->hmdf", gram, gram, precision=highest)
        mixer = coef_b * gram + coef_c * square
        current = coef_a * current + jnp.einsum(
            "hmfd,hmde->hmfe", current, mixer, precision=highest
        )
    return current


def orthogonalize(local_grads):
    grads = lax.psum(local_grads, "seq")
    norms = jnp.sqrt(jnp.sum(grads * grads, axis=(2, 3), keepdims=True))
    scaled = grads / (norms + tiny)
    return newton_schulz(scaled, gram_local(scaled), gram_local)


def body(queries, keys, values, token_rate, step_size, w_gate, w_up, w_down, w_out):
    token_count = queries.shape[1]
    rim_keys, rim_values = shifted(
        (keys[:, token_count - WIN :], values[:, token_count - WIN :]), "seq", 1
    )
    attended = window_attention(
        queries, keys, values, rim_keys, rim_values, lax.axis_index("seq") * token_count
    )
    gate_state, up_state, down_state = (w_gate, w_up, w_down)
    gate_copy = gate_state.astype(jnp.bfloat16)
    up_copy = up_state.astype(jnp.bfloat16)
    down_copy = down_state.astype(jnp.bfloat16)
    rate_scale = step_size[:, None, None]
    combined_parts = []
    for seg_index in range(SEGMENTS):
        local_grads = segment_gradients(
            keys[seg_index], values[seg_index], token_rate[seg_index], gate_copy, up_copy, down_copy
        )
        update = orthogonalize(local_grads)
        gate_state = gate_state - rate_scale * update[:, 0]
        up_state = up_state - rate_scale * update[:, 1]
        down_state = down_state - rate_scale * jnp.swapaxes(update[:, 2], 1, 2)
        gate_copy = gate_state.astype(jnp.bfloat16)
        up_copy = up_state.astype(jnp.bfloat16)
        down_copy = down_state.astype(jnp.bfloat16)
        fast_out = apply_fast(queries[seg_index], gate_copy, up_copy, down_copy)
        combined_parts.append((attended[seg_index] + fast_out).astype(jnp.bfloat16))
    combined = jnp.stack(combined_parts, axis=0)
    partial_out = jnp.einsum("ctw,wd->ctd", combined, w_out, preferred_element_type=jnp.float32)
    mixed = lax.psum_scatter(
        partial_out.astype(jnp.bfloat16), "head", scatter_dimension=2, tiled=True
    )
    return (mixed, gate_state, up_state, down_state)


def solution(mesh):
    return jax.shard_map(
        body,
        mesh=mesh,
        in_specs=(
            P(None, "seq", "head"),
            P(None, "seq", "head"),
            P(None, "seq", "head"),
            P(None, "head", "seq"),
            P("head"),
            P("head", None, None),
            P("head", None, None),
            P("head", None, None),
            P("head", None),
        ),
        out_specs=(
            P(None, "seq", "head"),
            P("head", None, None),
            P("head", None, None),
            P("head", None, None),
        ),
        check_vma=False,
    )
```

profile of v0, /device:TPU:1, one launch (start us, length us, event | category | flops | bytes accessed | tf_op | source)
XLA Modules:
  0.0 1321.4 jit_solution(3557505270199600091)
XLA Ops:
  15.1 2.8 reshape.127
  27.9 4.9 collective-permute-start
  41.2 2.8 reshape.128
  49.0 3.0 copy.77
  54.4 531.8 %all-reduce.3.cloned.1.call-done = f32[2,3,512,256]{3,2,0,1:T(8,128)} async-done(((f32[2,3,512,256]{3,2,0,1:T(8,128)}), f32[2,3,512,256]{3,2,0,1:T(8,128)}) %all-reduce.3.cloned.1.call-update) | async-done | bytes 3145744 | tf_op jit(solution)/shard_map/psum | solution.py:111
  589.1 5.4 fusion.20
  596.3 3.4 multiply_add_fusion.9
  599.7 5.3 fusion.18
  606.8 3.2 multiply_add_fusion.8
  610.0 5.4 fusion.16
  617.1 3.2 multiply_add_fusion.7
  620.3 5.6 fusion.14
  627.6 3.2 multiply_add_fusion.6
  630.8 5.1 fusion.12
  638.0 3.2 multiply_add_fusion.5
  651.1 2.8 fusion.61
  653.9 3.5 fusion.131
  665.2 2.9 fusion.108
  668.1 4.1 fusion.58
  674.7 532.3 %all-reduce.5.cloned.1.call-done = f32[2,3,512,256]{3,2,0,1:T(8,128)} async-done(((f32[2,3,512,256]{3,2,0,1:T(8,128)}), f32[2,3,512,256]{3,2,0,1:T(8,128)}) %all-reduce.5.cloned.1.call-update) | async-done | bytes 3145744 | tf_op jit(solution)/shard_map/psum | solution.py:111
  1209.8 5.4 fusion.10
  1217.0 3.8 multiply_add_fusion.4
  1220.9 5.1 fusion.8
  1227.8 3.3 multiply_add_fusion.3
  1231.1 5.1 fusion.6
  1238.1 3.2 multiply_add_fusion.2
  1241.3 5.4 fusion.4
  1248.4 3.2 multiply_add_fusion.1
  1251.6 5.4 fusion.2
  1258.8 3.2 multiply_add_fusion
  1266.5 4.0 fusion.59
  1280.1 34.3 %reduce-scatter.2.cloned.1.call-done = bf16[2,512,512]{2,1,0:T(8,128)(2,1)} async-done(((bf16[2,512,1024]{2,1,0:T(8,128)(2,1)}), bf16[2,512,512]{2,1,0:T(8,128)(2,1)}) %reduce-scatter.2.cloned.1.call-update) | async-done | bytes 1048592 | tf_op jit(solution)/shard_map/reduce_scatter | solution.py:146
  (122 shorter events, 91.3 us)
Async XLA Ops:
  7.2 1267.8 %copy-start = (bf16[512,1024]{1,0:T(8,128)(2,1)S(1)}, bf16[512,1024]{1,0:T(8,128)(2,1)}, u32[]{:S(2)}) copy-start(bf16[512,1024]{1,0:T(8,128)(2,1)} %param.17) | copy-start | bytes 3145732
  7.2 2.6 copy-start.7
  7.2 579.1 %all-reduce.3.cloned.1.call-start = ((), (), s32[]{:S(2)}) async-start(), calls=%async_computation.1 | async-start | bytes 6291456 | tf_op jit(solution)/shard_map/psum | solution.py:111
  9.7 3.7 copy-start.5
  9.7 1.9 copy-start.9
  11.6 1.8 copy-start.3
  13.4 4.5 copy-start.26
  17.9 2.2 copy-start.16
  17.9 2.5 copy-start.22
  20.5 2.7 copy-start.6
  20.5 2.7 copy-start.23
  27.0 1180.0 %all-reduce.5.cloned.1.call-start = ((), (), s32[]{:S(2)}) async-start(), calls=%async_computation.2 | async-start | bytes 6291456 | tf_op jit(solution)/shard_map/psum | solution.py:111
  27.1 8.5 copy-start.12
  27.9 18.7 %collective-permute-start = (bf16[2,256,512]{2,1,0:T(8,128)(2,1)}, bf16[2,256,512]{2,1,0:T(8,128)(2,1)}, u32[]{:S(2)}, u32[]{:S(2)}) collective-permute-start(bf16[2,256,512]{2,1,0:T(8,128)(2,1)} %slice.56), channel_id=1, source_target_pairs={{0,2},{2,4},{4,6},{6,8},{8,10},{10,12},{12,14},{14,16},{16,18},{18... | collective-permute-start | bytes 1572872 | tf_op jit(solution)/shard_map/ppermute | solution.py:24
  33.7 18.4 %collective-permute-start.1 = (bf16[2,256,512]{1,2,0:T(8,128)(2,1)}, bf16[2,256,512]{1,2,0:T(8,128)(2,1)}, u32[]{:S(2)}, u32[]{:S(2)}) collective-permute-start(bf16[2,256,512]{1,2,0:T(8,128)(2,1)} %slice.74), channel_id=1, source_target_pairs={{0,2},{2,4},{4,6},{6,8},{8,10},{10,12},{12,14},{14,16},{16,18},{18... | collective-permute-start | bytes 1572872 | tf_op jit(solution)/shard_map/ppermute | solution.py:24
  586.3 2.8 copy-start.20
  637.9 3.2 copy-start.8
  637.9 3.2 copy-start.10
  638.0 3.2 copy-start.27
  641.2 1.0 copy-start.4
  642.7 1.2 copy-start.17
  643.9 1.5 copy-start.13
  651.0 663.4 %reduce-scatter.2.cloned.1.call-start = ((), (), s32[]{:S(2)}) async-start(), calls=%async_computation.3 | async-start | bytes 3145728 | tf_op jit(solution)/shard_map/reduce_scatter | solution.py:146
  653.9 3.5 copy-start.25
  1207.0 2.8 copy-start.21
  1261.9 1.3 copy-start.2
  1263.2 3.2 copy-start.11
  1263.2 1.4 copy-start.24
  1263.5 3.0 copy-start.18
  1270.4 2.7 copy-start.14
  1270.4 2.7 copy-start.15
  1277.6 1.2 copy-start.19
  (1 other events, 1.0 us)
Sparse Core Ops, SparseCore 0:
  27.2 559.0 all-reduce.2
  651.2 555.7 all-reduce.4
  1277.8 36.6 reduce-scatter.1
where the time goes:
time: 1330 us; the launch traced here: 1320 us
  waiting for transfers between devices  1100 us (83%)
  matrix products  138 us (10%)
  local copies, waits for them, and re-layouts  40 us (3%)
  other arithmetic  23 us (2%)
  between operations  14.8 us (1%)
    psum x2, waiting for transfers between devices, orthogonalize(): grads = lax.psum(local_grads, 'seq')  1060 us
    dot_general x10, matrix products, gram_local(): return jnp.einsum('hmfd,hmfe->hmde', rows, rows, precision=highest)  53.2 us
    reduce_scatter x1, waiting for transfers between devices, body(): lax.psum_scatter(partial_out.astype(jnp.bfloat16), 'head', scatter_dimens...  34.3 us
    dot_general x10, matrix products, newton_schulz(): jnp.einsum('hmfd,hmde->hmfe', current, mixer, precision=highest)  32.8 us
  transfers between devices with their start and end apart: 5, of which 3 were waited for; matrix products, arithmetic and copies ran while one was open for 3% of the time, Pallas kernels for 0%

commit v1 on v0

v1 whole, which is shorter than its diff:
```python
import functools

import jax
import jax.numpy as jnp
from jax import lax
from jax.experimental import pallas as pl
from jax.experimental.pallas import tpu as pltpu
from jax.sharding import PartitionSpec as P

F32 = jnp.float32
BF = jnp.bfloat16
MESH = pl.DeviceIdType.MESH

DH = 256
FH = 512
WIN = 256
T = 512
TC = 2 * T
SEG = 2
BLK = 256
coef_a = 3.4445
coef_b = -4.775
coef_c = 2.0315
tiny = 1e-07

SINGLE_STEPS = 3
SPLIT_STEPS = 2


def nn(a, b):
    return jnp.dot(a, b, preferred_element_type=F32)


def nt(a, b):
    return lax.dot_general(a, b, (((1,), (1,)), ((), ())), preferred_element_type=F32)


def tn(a, b):
    return lax.dot_general(a, b, (((0,), (0,)), ((), ())), preferred_element_type=F32)


def sigmoid(v):
    return 1.0 / (1.0 + jnp.exp(-v))


def split(a):
    high = a.astype(BF)
    return high, (a - high.astype(F32)).astype(BF)


def kernel(
    q_ref, k_ref, v_ref, rate_ref, step_ref, wg_ref, wu_ref, wd_ref, wo_ref,
    mixed_ref, gate_ref, up_ref, down_ref,
    qb, kb, vb, rates, rate_send, w, wb, wdb, wo, act, d1, d3, g32, gb, rsr, arb, gf, xs,
    att, cs, cb, zs, zo, zr, mx,
    loc_sem, w_sem, wo_sem, d2d_s, d2d_r, rate_s, rate_r, halo_s, halo_r,
    rs_s, rs_r, ar_s, ar_r, ag_s, ag_r, cs_s, cs_r, zs_s, zs_r, st_s, st_r, out_sem,
):
    seq = lax.axis_index("seq")
    hg = lax.axis_index("head")
    c = lax.rem(seq, 2)
    z = lax.rem(seq // 2, 2)
    y = lax.rem(seq // 4, 4)
    x = seq // 16
    oc = 1 - c
    chip = seq // 2

    def at(px, py, pz, pc=None):
        return {"seq": ((px * 4 + py) * 2 + pz) * 2 + (c if pc is None else pc)}

    sibling = at(x, y, z, oc)
    across = {"head": 1 - hg}
    next_chip = {"seq": lax.rem(chip + 1, 32) * 2 + c}
    prev_chip = {"seq": lax.rem(chip + 31, 32) * 2 + c}

    def group8(m, k):
        r, b = k // 2, k % 2
        if m == 0:
            py, pz = lax.rem(y + r, 4), lax.rem(z + b, 2)
            return at(x, py, pz), py * 2 + pz
        if m == 1:
            px, pz = lax.rem(x + r, 4), lax.rem(z + b, 2)
            return at(px, y, pz), px * 2 + pz
        px = lax.rem(x + r, 4)
        py = y + b * (1 - 2 * lax.rem(y, 2))
        return at(px, py, z), px * 2 + lax.rem(py, 2)

    def group4(m, k):
        if m == 0:
            px = lax.rem(x + k, 4)
            return at(px, y, z), px
        if m == 1:
            py = lax.rem(y + k, 4)
            return at(x, py, z), py
        py, pz = lax.rem(y + 2 * (k // 2), 4), lax.rem(z + k % 2, 2)
        return at(x, py, pz), (py // 2) * 2 + pz

    def remote(src, dst, ss, rs, device):
        return pltpu.make_async_remote_copy(
            src_ref=src, dst_ref=dst, send_sem=ss, recv_sem=rs, device_id=device, device_id_type=MESH
        )

    barrier = pltpu.get_barrier_semaphore()
    senders = [group8(0, k)[0] for k in range(1, 8)]
    senders += [group8(1, k)[0] for k in range(2, 8)]
    senders += [group8(2, k)[0] for k in (3, 5, 7)]
    senders += [sibling, across, prev_chip]
    for device in senders:
        pl.semaphore_signal(barrier, inc=1, device_id=device, device_id_type=MESH)

    my_cols = pl.ds(pl.multiple_of(c * DH, DH), DH)
    other_cols = pl.ds(pl.multiple_of(oc * DH, DH), DH)
    my_rows = pl.ds(pl.multiple_of(c * T, T), T)
    my_halo_rows = pl.ds(pl.multiple_of(WIN + c * T, WIN), T)

    def place(i, s):
        return (kb.at[s, my_halo_rows], vb.at[s, my_halo_rows], qb.at[s, my_rows])[i]

    inputs = (k_ref, v_ref, q_ref)

    def local_in(i, s):
        return pltpu.make_async_copy(inputs[i].at[s, :, my_cols], place(i, s), loc_sem.at[i, s])

    def to_sibling(i, s):
        return remote(
            inputs[i].at[s, :, other_cols], place(i, s), d2d_s.at[i, s], d2d_r.at[i, s], sibling
        )

    w_copies = [
        pltpu.make_async_copy(wg_ref.at[c], w.at[0], w_sem.at[0]),
        pltpu.make_async_copy(wu_ref.at[c], w.at[1], w_sem.at[1]),
        pltpu.make_async_copy(wd_ref.at[c], wdb, w_sem.at[2]),
    ]
    wo_copies = [
        pltpu.make_async_copy(wo_ref.at[:, pl.ds(i * 512, 512)], wo.at[i], wo_sem.at[i]) for i in range(2)
    ]
    local_in(0, 0).start()
    w_copies[0].start()
    w_copies[1].start()
    w_copies[2].start()
    local_in(1, 0).start()
    local_in(0, 1).start()
    local_in(1, 1).start()
    local_in(2, 0).start()
    local_in(2, 1).start()
    wo_copies[0].start()
    wo_copies[1].start()

    rate_send[...] = jnp.zeros_like(rate_send)
    for s in range(SEG):
        both = rate_ref[s]
        rates[c, s : s + 1, :] = jnp.where(c == 0, both[0:1], both[1:2])
        rate_send[s : s + 1, :] = jnp.where(c == 0, both[1:2], both[0:1])
    rate_copy = remote(rate_send, rates.at[c], rate_s, rate_r, sibling)

    w_copies[0].wait()
    wb[0] = w[0].astype(BF)
    w_copies[1].wait()
    wb[1] = w[1].astype(BF)
    w_copies[2].wait()
    w[2] = wdb[...].T
    wb[2] = w[2].astype(BF)

    def forward(s, half, j):
        start = pl.multiple_of(half * T + j * BLK, BLK)
        rows = pl.ds(pl.multiple_of(WIN + start, BLK), BLK)
        cols = pl.ds(start, BLK)
        key = kb[s, rows, :]
        value = vb[s, rows, :]
        rate = -rates[half, s : s + 1, pl.ds(pl.multiple_of(j * BLK, BLK), BLK)]
        g1 = nt(wb[0], key)
        g3 = nt(wb[1], key)
        back = nt(wb[2], value) * rate
        sg = sigmoid(g1)
        ga = g1 * sg
        act[:, cols] = (ga * g3 * rate).astype(BF)
        d1[:, cols] = (back * g3 * (sg + ga * (1.0 - sg))).astype(BF)
        d3[:, cols] = (back * ga).astype(BF)

    def rs(s, m, k):
        device, p = group8(m, k)
        return remote(gb.at[s, m, p], rsr.at[s, m, k - 1], rs_s.at[s, m, k - 1], rs_r.at[s, m, k - 1], device)

    def ar(s, m, k):
        mine = group4(m, 0)[1]
        ref = arb.at[s, m, mine]
        return remote(ref, ref, ar_s.at[s, m, k - 1], ar_r.at[s, m, k - 1], group4(m, k)[0])

    def ag(s, m, k):
        ref = gf.at[s, m, group8(m, 0)[1]]
        return remote(ref, ref, ag_s.at[s, m, k - 1], ag_r.at[s, m, k - 1], group8(m, k)[0])

    far_first = (5, 4, 3, 7, 2, 6, 1)
    order = (2, 0, 1)

    def gradients(s):
        keys = kb[s, pl.ds(WIN, TC), :]
        values = vb[s, pl.ds(WIN, TC), :]
        for m in order:
            grad = nn(act[...], values) if m == 2 else nn((d1, d3)[m][...], keys)
            for p in range(8):
                part = grad[p * 64 : (p + 1) * 64]
                g32[m, p] = part
                gb[s, m, p] = part.astype(BF)
            for k in far_first:
                rs(s, m, k).start()

    def reduce(s):
        for m in order:
            for k in far_first:
                rs(s, m, k).wait()
            total = g32[m, group8(m, 0)[1]]
            for k in range(1, 8):
                total = total + rsr[s, m, k - 1].astype(F32)
            arb[s, m, group4(m, 0)[1]] = total.astype(BF)
            for k in (2, 1, 3):
                ar(s, m, k).start()

    def spread(s):
        for m in order:
            for k in (1, 3, 2):
                ar(s, m, k).wait()
            total = arb[s, m, 0].astype(F32)
            for a in range(1, 4):
                total = total + arb[s, m, a].astype(F32)
            gf[s, m, group8(m, 0)[1]] = total.astype(BF)
            for k in far_first:
                ag(s, m, k).start()

    def update(s):
        for m in order:
            for k in far_first:
                ag(s, m, k).wait()
            rows = gf[s, m].reshape(FH, DH).astype(F32)
            norm = jnp.sqrt(jnp.sum(rows * rows, keepdims=True))
            xs[m] = rows * (1.0 / (norm + tiny))

        def single(_, carry):
            for m in order:
                cur = xs[m]
                low = cur.astype(BF)
                gram = tn(low, low)
                gram_b = gram.astype(BF)
                mixer = coef_b * gram + coef_c * nn(gram_b, gram_b)
                xs[m] = coef_a * cur + nn(low, mixer.astype(BF))
            return carry

        def double(_, carry):
            for m in order:
                cur = xs[m]
                hi, lo = split(cur)
                gram = tn(hi, hi) + (tn(hi, lo) + tn(lo, hi))
                gh, gl = split(gram)
                square = nn(gh, gh) + (nn(gh, gl) + nn(gl, gh))
                mh, ml = split(coef_b * gram + coef_c * square)
                xs[m] = coef_a * cur + (nn(hi, mh) + (nn(hi, ml) + nn(lo, mh)))
            return carry

        lax.fori_loop(0, SINGLE_STEPS, single, 0)
        lax.fori_loop(0, SPLIT_STEPS, double, 0)
        step = step_ref[c]
        for m in range(3):
            new = w[m] - step * xs[m]
            w[m] = new
            wb[m] = new.astype(BF)

    row_ids = lax.broadcasted_iota(jnp.int32, (BLK, 2 * BLK), 0)
    col_ids = lax.broadcasted_iota(jnp.int32, (BLK, 2 * BLK), 1)

    def attention(s, j):
        start = pl.multiple_of(j * BLK, BLK)
        query = qb[s, pl.ds(start, BLK), :]
        key = kb[s, pl.ds(start, 2 * BLK), :]
        value = vb[s, pl.ds(start, 2 * BLK), :]
        scores = nt(query, key) * (1.0 / 16.0)
        least = jnp.where(jnp.logical_and(chip == 0, j == 0), WIN, 0)
        allowed = (col_ids > row_ids) & (col_ids <= row_ids + WIN) & (col_ids >= least)
        scores = jnp.where(allowed, scores, -1e30)
        top = jnp.max(scores, axis=-1, keepdims=True)
        weights = jnp.exp(scores - top)
        total = jnp.sum(weights, axis=-1, keepdims=True)
        att[s, pl.ds(start, BLK), :] = nn(weights.astype(BF), value) / total

    def attend(s, first, last):
        def one(j, carry):
            attention(s, j)
            return carry

        lax.fori_loop(first, last, one, 0)

    def fast(s, half, j):
        start = pl.multiple_of(half * T + j * BLK, BLK)
        query = qb[s, pl.ds(start, BLK), :]
        g1 = nt(query, wb[0])
        g3 = nt(query, wb[1])
        hidden = (g1 * sigmoid(g1) * g3).astype(BF)
        return (att[s, pl.ds(start, BLK), :] + nn(hidden, wb[2])).astype(BF)

    def part(j):
        return pl.ds(j * BLK, BLK)

    def cs_copy(s, j):
        return remote(cs.at[s, part(j)], cb.at[s, c, part(j)], cs_s.at[s, j], cs_r.at[s, j], sibling)

    def z_copy(s, j):
        return remote(zs.at[s, part(j)], zr.at[s, part(j)], zs_s.at[s, j], zs_r.at[s, j], across)

    def project(s, j, group):
        return (
            nn(cb[s, 0, part(j)], wo[group, 0:DH, :]) + nn(cb[s, 1, part(j)], wo[group, DH : 2 * DH, :])
        ).astype(BF)

    def apply(s):
        for j in range(2):
            cs[s, part(j)] = fast(s, oc, j)
            cs_copy(s, j).start()
        for j in range(2):
            cb[s, c, part(j)] = fast(s, c, j)
            cs_copy(s, j).wait_recv()
            zs[s, part(j)] = project(s, j, 1 - hg)
            z_copy(s, j).start()
        for j in range(2):
            cs_copy(s, j).wait_send()
            zo[s, part(j)] = project(s, j, hg)

    def out_copy(s):
        return pltpu.make_async_copy(mx.at[s], mixed_ref.at[s], out_sem.at[s])

    def finish(s):
        for j in range(2):
            z_copy(s, j).wait()
            mx[s, part(j)] = (zo[s, part(j)].astype(F32) + zr[s, part(j)].astype(F32)).astype(BF)
        out_copy(s).start()

    local_in(0, 0).wait()
    local_in(1, 0).wait()
    forward(0, c, 0)
    pl.semaphore_wait(barrier, len(senders))
    to_sibling(0, 0).start()
    to_sibling(1, 0).start()
    rate_copy.start()
    for i, s in ((0, 1), (1, 1), (2, 0), (2, 1)):
        to_sibling(i, s).start()
    forward(0, c, 1)
    to_sibling(0, 0).wait()
    to_sibling(1, 0).wait()
    rate_copy.wait()
    forward(0, oc, 0)
    forward(0, oc, 1)
    gradients(0)

    def halo(i, s):
        buf = (kb, vb)[i]
        return remote(
            buf.at[s, pl.ds(TC, WIN)], buf.at[s, pl.ds(0, WIN)], halo_s.at[i, s], halo_r.at[i, s], next_chip
        )

    halo(0, 0).start()
    halo(1, 0).start()
    for i in range(3):
        local_in(i, 1).wait()
        to_sibling(i, 1).wait()
    local_in(2, 0).wait()
    to_sibling(2, 0).wait()
    halo(0, 1).start()
    halo(1, 1).start()
    for i in range(2):
        wo_copies[i].wait()

    reduce(0)
    halo(0, 0).wait()
    halo(1, 0).wait()
    attend(0, 0, 4)
    spread(0)
    halo(0, 1).wait()
    halo(1, 1).wait()
    attend(1, 0, 4)
    update(0)

    for j in range(2):
        forward(1, c, j)
        forward(1, oc, j)
    gradients(1)
    apply(0)
    reduce(1)
    spread(1)
    finish(0)
    update(1)
    apply(1)

    outs = (gate_ref.at[c], up_ref.at[c], down_ref.at[c])
    wdb[...] = w[2].T
    sources = (w.at[0], w.at[1], wdb)
    for m in range(3):
        remote(sources[m], outs[m], st_s.at[m], st_r.at[m], sibling).start()
        pltpu.make_async_copy(sources[m], outs[m], w_sem.at[m]).start()
    finish(1)
    for m in range(3):
        remote(sources[m], outs[m], st_s.at[m], st_r.at[m], sibling).wait()
        pltpu.make_async_copy(sources[m], outs[m], w_sem.at[m]).wait()
    for s in range(SEG):
        out_copy(s).wait()


def body(queries, keys, values, token_rate, step_size, w_gate, w_up, w_down, w_out):
    dma = pltpu.SemaphoreType.DMA
    anywhere = pl.BlockSpec(memory_space=pl.ANY)

    def b16(*shape):
        return pltpu.VMEM(shape, BF)

    def f32(*shape):
        return pltpu.VMEM(shape, F32)

    return pl.pallas_call(
        kernel,
        out_shape=(
            jax.ShapeDtypeStruct((SEG, T, 2 * DH), BF),
            jax.ShapeDtypeStruct((2, FH, DH), F32),
            jax.ShapeDtypeStruct((2, FH, DH), F32),
            jax.ShapeDtypeStruct((2, DH, FH), F32),
        ),
        in_specs=[
            anywhere, anywhere, anywhere,
            pl.BlockSpec(memory_space=pltpu.VMEM),
            pl.BlockSpec(memory_space=pltpu.SMEM),
            anywhere, anywhere, anywhere, anywhere,
        ],
        out_specs=(anywhere, anywhere, anywhere, anywhere),
        scratch_shapes=[
            b16(SEG, TC, DH), b16(SEG, WIN + TC, DH), b16(SEG, WIN + TC, DH),
            f32(2, 8, T), f32(8, T),
            f32(3, FH, DH), b16(3, FH, DH), f32(DH, FH), b16(2, 512, 512),
            b16(FH, TC), b16(FH, TC), b16(FH, TC),
            f32(3, 8, 64, DH), b16(SEG, 3, 8, 64, DH), b16(SEG, 3, 7, 64, DH), b16(SEG, 3, 4, 64, DH),
            b16(SEG, 3, 8, 64, DH), f32(3, FH, DH),
            f32(SEG, TC, DH), b16(SEG, T, DH), b16(SEG, 2, T, DH),
            b16(SEG, T, 512), b16(SEG, T, 512), b16(SEG, T, 512), b16(SEG, T, 512),
            dma((3, 2)), dma((3,)), dma((2,)), dma((3, 2)), dma((3, 2)), dma, dma, dma((2, 2)), dma((2, 2)),
            dma((2, 3, 7)), dma((2, 3, 7)), dma((2, 3, 3)), dma((2, 3, 3)), dma((2, 3, 7)), dma((2, 3, 7)),
            dma((2, 2)), dma((2, 2)), dma((2, 2)), dma((2, 2)), dma((3,)), dma((3,)), dma((2,)),
        ],
        compiler_params=pltpu.CompilerParams(
            collective_id=0, has_side_effects=True, vmem_limit_bytes=56 * 2**20
        ),
        name="layer",
    )(queries, keys, values, token_rate, step_size, w_gate, w_up, w_down, w_out)


def solution(mesh):
    return jax.shard_map(
        body,
        mesh=mesh,
        in_specs=(
            P(None, "seq", "head"),
            P(None, "seq", "head"),
            P(None, "seq", "head"),
            P(None, "head", "seq"),
            P("head"),
            P("head", None, None),
            P("head", None, None),
            P("head", None, None),
            P("head", None),
        ),
        out_specs=(
            P(None, "seq", "head"),
            P("head", None, None),
            P("head", None, None),
            P("head", None, None),
        ),
        check_vma=False,
    )
```

time: 1330 us -> 123 us (0.09)
  waiting for transfers between devices: 1100 us -> 0 us
  matrix products: 138 us -> 0 us
  Pallas kernels: 0 us -> 116 us
  local copies, waits for them, and re-layouts: 40 us -> 6.53 us
  other arithmetic: 23 us -> 0 us
  between operations: 14.8 us -> 0.65 us
    psum x2 -> x0, waiting for transfers between devices: 1060 us -> none  [orthogonalize(): grads = lax.psum(local_grads, 'seq')]
    dot_general x49 -> x0, matrix products: 138 us -> none  [the longest x10 53.2 us: gram_local(): return jnp.einsum('hmfd,hmfe->hmde', rows, rows, precision=highest)]
    pallas_call x0 -> x1, Pallas kernels: none -> 116 us  [body(): pl.pallas_call(kernel, out_shape=(jax.ShapeDtypeStruct((SEG, T, 2 * DH),...]
    reduce_scatter x1 -> x0, waiting for transfers between devices: 34.3 us -> none  [body(): lax.psum_scatter(partial_out.astype(jnp.bfloat16), 'head', scatter_dimens...]
  transfers between devices with their start and end apart: 5 -> 0, of which waited for: 3 -> 0; matrix products, arithmetic and copies ran while one was open for 3% -> 0% of each run, Pallas kernels for 0% -> 0%
where the time goes in v1:
time: 123 us
  Pallas kernels  116 us (94%)
  local copies, waits for them, and re-layouts  6.53 us (5%)
    pallas_call x1, Pallas kernels, body(): pl.pallas_call(kernel, out_shape=(jax.ShapeDtypeStruct((SEG, T, 2 * DH),...  116 us
    unnamed x10, local copies, waits for them, and re-layouts  6.53 us

profile of v1, /device:TPU:1, one launch (start us, length us, event | category | flops | bytes accessed | tf_op | source)
XLA Modules:
  0.0 123.1 jit_solution(8156008973489579625)
XLA Ops:
  0.6 115.9 %layer.1 = (bf16[2,512,512]{2,1,0:T(8,128)(2,1)}, f32[2,512,256]{2,1,0:T(8,128)}, f32[2,512,256]{2,1,0:T(8,128)}, f32[2,256,512]{2,1,0:T(8,128)}) custom-call(bf16[2,512,512]{2,1,0:T(8,128)(2,1)} %q_ref.1, bf16[2,512,512]{2,1,0:T(8,128)(2,1)} %k_ref.1, bf16[2,512,512]{2,1,0:T(8,128)(2,1)} %v_ref.1, f32[2,2,512]{2,1,0:T(2,128)} %rate_ref.1, f32[2]{0:T(128)} %step_ref.1, ...), custom_call_target="tpu_custom_call" | custom-call | tf_op jit(solution)/shard_map/layer/pallas_call | solution.py:415
  116.5 0.0 copy-start.2
  116.5 2.4 %copy.17 = bf16[2,512,512]{2,1,0:T(8,128)(2,1)} copy(bf16[2,512,512]{2,1,0:T(8,128)(2,1)} %get-tuple-element.8) | data formatting | bytes 2097152
  118.9 0.0 copy-done.2
  118.9 0.0 copy-start.1
  118.9 1.0 copy.18
  119.9 0.6 copy-done.1
  120.5 0.0 copy-start
  120.5 1.0 copy.19
  121.5 0.6 copy-done
  122.1 1.0 copy.20
Async XLA Ops:
  116.5 2.4 %copy-start.2 = (f32[2,512,256]{2,1,0:T(8,128)S(1)}, f32[2,512,256]{2,1,0:T(8,128)}, u32[]{:S(2)}) copy-start(f32[2,512,256]{2,1,0:T(8,128)} %get-tuple-element.9) | copy-start | bytes 3145732
  118.9 1.6 %copy-start.1 = (f32[2,512,256]{2,1,0:T(8,128)S(1)}, f32[2,512,256]{2,1,0:T(8,128)}, u32[]{:S(2)}) copy-start(f32[2,512,256]{2,1,0:T(8,128)} %get-tuple-element.10) | copy-start | bytes 3145732
  120.5 1.6 %copy-start = (f32[2,256,512]{2,1,0:T(8,128)S(1)}, f32[2,256,512]{2,1,0:T(8,128)}, u32[]{:S(2)}) copy-start(f32[2,256,512]{2,1,0:T(8,128)} %get-tuple-element.11) | copy-start | bytes 3145732

commit v2 on v1

--- a/solution.py
+++ b/solution.py
@@ -26,6 +26,8 @@
 SINGLE_STEPS = 3
 SPLIT_STEPS = 2
 
+JOBS = ((2, 0, 2, 0, 0), (0, 0, 2, 1, 0), (1, 0, 1, 0, 1), (1, 8, 1, 1, 1))
+
 
 def nn(a, b):
     return jnp.dot(a, b, preferred_element_type=F32)
@@ -51,9 +53,9 @@
 def kernel(
     q_ref, k_ref, v_ref, rate_ref, step_ref, wg_ref, wu_ref, wd_ref, wo_ref,
     mixed_ref, gate_ref, up_ref, down_ref,
-    qb, kb, vb, rates, rate_send, w, wb, wdb, wo, act, d1, d3, g32, gb, rsr, arb, gf, xs,
+    qb, kb, vb, rates, rate_in, rate_send, w, wb, wdb, wo, act, d1, d3, g32, gb, rsr, arb, gf,
     att, cs, cb, zs, zo, zr, mx,
-    loc_sem, w_sem, wo_sem, d2d_s, d2d_r, rate_s, rate_r, halo_s, halo_r,
+    loc_sem, w_sem, wo_sem, rate_l, d2d_s, d2d_r, rate_s, rate_r, halo_s, halo_r,
     rs_s, rs_r, ar_s, ar_r, ag_s, ag_r, cs_s, cs_r, zs_s, zs_r, st_s, st_r, out_sem,
 ):
     seq = lax.axis_index("seq")
@@ -73,27 +75,25 @@
     next_chip = {"seq": lax.rem(chip + 1, 32) * 2 + c}
     prev_chip = {"seq": lax.rem(chip + 31, 32) * 2 + c}
 
-    def group8(m, k):
+    def group8(job, k):
+        _, _, _, line, shift = JOBS[job]
         r, b = k // 2, k % 2
-        if m == 0:
-            py, pz = lax.rem(y + r, 4), lax.rem(z + b, 2)
-            return at(x, py, pz), py * 2 + pz
-        if m == 1:
-            px, pz = lax.rem(x + r, 4), lax.rem(z + b, 2)
-            return at(px, y, pz), px * 2 + pz
-        px = lax.rem(x + r, 4)
-        py = y + b * (1 - 2 * lax.rem(y, 2))
-        return at(px, py, z), px * 2 + lax.rem(py, 2)
-
-    def group4(m, k):
-        if m == 0:
-            px = lax.rem(x + k, 4)
-            return at(px, y, z), px
-        if m == 1:
-            py = lax.rem(y + k, 4)
-            return at(x, py, z), py
-        py, pz = lax.rem(y + 2 * (k // 2), 4), lax.rem(z + k % 2, 2)
-        return at(x, py, pz), (py // 2) * 2 + pz
+        along, beside = (x, y) if line else (y, x)
+        bit = lax.rem(beside + shift, 2)
+        along = lax.rem(along + r, 4)
+        beside = lax.rem(beside + b * (1 - 2 * bit) + 4, 4)
+        px, py = (along, beside) if line else (beside, along)
+        return at(px, py, z), along * 2 + lax.rem(bit + b, 2)
+
+    def group4(job, k):
+        _, _, _, line, shift = JOBS[job]
+        beside, pz = lax.rem((y if line else x) + 2 * (k // 2), 4), lax.rem(z + k % 2, 2)
+        index = (lax.rem(beside + shift, 4) // 2) * 2 + pz
+        return (at(x, beside, pz) if line else at(beside, y, pz)), index
+
+    def piece(job, p):
+        _, first, rows, _, _ = JOBS[job]
+        return pl.ds(first + p * rows, rows)
 
     def remote(src, dst, ss, rs, device):
         return pltpu.make_async_remote_copy(
@@ -101,9 +101,9 @@
         )
 
     barrier = pltpu.get_barrier_semaphore()
-    senders = [group8(0, k)[0] for k in range(1, 8)]
-    senders += [group8(1, k)[0] for k in range(2, 8)]
-    senders += [group8(2, k)[0] for k in (3, 5, 7)]
+    offsets = [(i, j, 0) for i in range(4) for j in range(4) if (i, j) not in ((0, 0), (2, 2))]
+    offsets += [(0, 0, 1), (0, 2, 1), (2, 0, 1)]
+    senders = [at(lax.rem(x + i, 4), lax.rem(y + j, 4), lax.rem(z + k, 2)) for i, j, k in offsets]
     senders += [sibling, across, prev_chip]
     for device in senders:
         pl.semaphore_signal(barrier, inc=1, device_id=device, device_id_type=MESH)
@@ -134,6 +134,8 @@
     wo_copies = [
         pltpu.make_async_copy(wo_ref.at[:, pl.ds(i * 512, 512)], wo.at[i], wo_sem.at[i]) for i in range(2)
     ]
+    rate_load = pltpu.make_async_copy(rate_ref, rate_in, rate_l)
+    rate_load.start()
     local_in(0, 0).start()
     w_copies[0].start()
     w_copies[1].start()
@@ -147,8 +149,9 @@
     wo_copies[1].start()
 
     rate_send[...] = jnp.zeros_like(rate_send)
+    rate_load.wait()
     for s in range(SEG):
-        both = rate_ref[s]
+        both = rate_in[s]
         rates[c, s : s + 1, :] = jnp.where(c == 0, both[0:1], both[1:2])
         rate_send[s : s + 1, :] = jnp.where(c == 0, both[1:2], both[0:1])
     rate_copy = remote(rate_send, rates.at[c], rate_s, rate_r, sibling)
@@ -157,10 +160,6 @@
     wb[0] = w[0].astype(BF)
     w_copies[1].wait()
     wb[1] = w[1].astype(BF)
-    w_copies[2].wait()
-    w[2] = wdb[...].T
-    wb[2] = w[2].astype(BF)
-
     def forward(s, half, j):
         start = pl.multiple_of(half * T + j * BLK, BLK)
         rows = pl.ds(pl.multiple_of(WIN + start, BLK), BLK)
@@ -177,18 +176,24 @@
         d1[:, cols] = (back * g3 * (sg + ga * (1.0 - sg))).astype(BF)
         d3[:, cols] = (back * ga).astype(BF)
 
-    def rs(s, m, k):
-        device, p = group8(m, k)
-        return remote(gb.at[s, m, p], rsr.at[s, m, k - 1], rs_s.at[s, m, k - 1], rs_r.at[s, m, k - 1], device)
-
-    def ar(s, m, k):
-        mine = group4(m, 0)[1]
-        ref = arb.at[s, m, mine]
-        return remote(ref, ref, ar_s.at[s, m, k - 1], ar_r.at[s, m, k - 1], group4(m, k)[0])
-
-    def ag(s, m, k):
-        ref = gf.at[s, m, group8(m, 0)[1]]
-        return remote(ref, ref, ag_s.at[s, m, k - 1], ag_r.at[s, m, k - 1], group8(m, k)[0])
+    def rs(s, job, k):
+        m, rows = JOBS[job][0], JOBS[job][2]
+        device, p = group8(job, k)
+        return remote(
+            gb.at[s, m, piece(job, p)],
+            rsr.at[s, job, k - 1, pl.ds(0, rows)],
+            rs_s.at[s, job, k - 1],
+            rs_r.at[s, job, k - 1],
+            device,
+        )
+
+    def ar(s, job, k):
+        ref = arb.at[s, job, group4(job, 0)[1], pl.ds(0, JOBS[job][2])]
+        return remote(ref, ref, ar_s.at[s, job, k - 1], ar_r.at[s, job, k - 1], group4(job, k)[0])
+
+    def ag(s, job, k):
+        ref = gf.at[s, JOBS[job][0], piece(job, group8(job, 0)[1])]
+        return remote(ref, ref, ag_s.at[s, job, k - 1], ag_r.at[s, job, k - 1], group8(job, k)[0])
 
     far_first = (5, 4, 3, 7, 2, 6, 1)
     order = (2, 0, 1)
@@ -198,69 +203,68 @@
         values = vb[s, pl.ds(WIN, TC), :]
         for m in order:
             grad = nn(act[...], values) if m == 2 else nn((d1, d3)[m][...], keys)
-            for p in range(8):
-                part = grad[p * 64 : (p + 1) * 64]
-                g32[m, p] = part
-                gb[s, m, p] = part.astype(BF)
+            grad = grad.reshape(16, 32, DH)
+            g32[m] = grad
+            gb[s, m] = grad.astype(BF)
             for k in far_first:
-                rs(s, m, k).start()
+                for job in range(4):
+                    if JOBS[job][0] == m:
+                        rs(s, job, k).start()
 
     def reduce(s):
-        for m in order:
+        for job in range(4):
+            m, rows = JOBS[job][0], JOBS[job][2]
             for k in far_first:
-                rs(s, m, k).wait()
-            total = g32[m, group8(m, 0)[1]]
+                rs(s, job, k).wait()
+            total = g32[m, piece(job, group8(job, 0)[1])]
             for k in range(1, 8):
-                total = total + rsr[s, m, k - 1].astype(F32)
-            arb[s, m, group4(m, 0)[1]] = total.astype(BF)
-            for k in (2, 1, 3):
-                ar(s, m, k).start()
+                total = total + rsr[s, job, k - 1, 0:rows].astype(F32)
+            arb[s, job, group4(job, 0)[1], 0:rows] = total.astype(BF)
+            for k in (3, 2, 1):
+                ar(s, job, k).start()
 
     def spread(s):
-        for m in order:
-            for k in (1, 3, 2):
-                ar(s, m, k).wait()
-            total = arb[s, m, 0].astype(F32)
+        for job in range(4):
+            m, rows = JOBS[job][0], JOBS[job][2]
+            for k in (1, 2, 3):
+                ar(s, job, k).wait()
+            total = arb[s, job, 0, 0:rows].astype(F32)
             for a in range(1, 4):
-                total = total + arb[s, m, a].astype(F32)
-            gf[s, m, group8(m, 0)[1]] = total.astype(BF)
+                total = total + arb[s, job, a, 0:rows].astype(F32)
+            gf[s, m, piece(job, group8(job, 0)[1])] = total.astype(BF)
             for k in far_first:
-                ag(s, m, k).start()
+                ag(s, job, k).start()
+
+    def arrive(s):
+        for job in range(4):
+            for k in far_first:
+                ag(s, job, k).wait()
 
     def update(s):
-        for m in order:
-            for k in far_first:
-                ag(s, m, k).wait()
+        cur = []
+        for m in range(3):
             rows = gf[s, m].reshape(FH, DH).astype(F32)
             norm = jnp.sqrt(jnp.sum(rows * rows, keepdims=True))
-            xs[m] = rows * (1.0 / (norm + tiny))
-
-        def single(_, carry):
-            for m in order:
-                cur = xs[m]
-                low = cur.astype(BF)
-                gram = tn(low, low)
-                gram_b = gram.astype(BF)
-                mixer = coef_b * gram + coef_c * nn(gram_b, gram_b)
-                xs[m] = coef_a * cur + nn(low, mixer.astype(BF))
-            return carry
-
-        def double(_, carry):
-            for m in order:
-                cur = xs[m]
-                hi, lo = split(cur)
-                gram = tn(hi, hi) + (tn(hi, lo) + tn(lo, hi))
-                gh, gl = split(gram)
-                square = nn(gh, gh) + (nn(gh, gl) + nn(gl, gh))
-                mh, ml = split(coef_b * gram + coef_c * square)
-                xs[m] = coef_a * cur + (nn(hi, mh) + (nn(hi, ml) + nn(lo, mh)))
-            return carry
-
-        lax.fori_loop(0, SINGLE_STEPS, single, 0)
-        lax.fori_loop(0, SPLIT_STEPS, double, 0)
+            cur.append(rows * (1.0 / (norm + tiny)))
+        for i in range(SINGLE_STEPS + SPLIT_STEPS):
+            high = [a.astype(BF) for a in cur]
+            gram = [tn(a, a) for a in high]
+            if i < SINGLE_STEPS:
+                gram_b = [a.astype(BF) for a in gram]
+                square = [nn(a, a) for a in gram_b]
+                mixer = [(coef_b * a + coef_c * b).astype(BF) for a, b in zip(gram, square)]
+                change = [nn(a, b) for a, b in zip(high, mixer)]
+            else:
+                parts = [split(a) for a in gram]
+                cross = [nn(a, b) for a, b in parts]
+                square = [nn(a, a) + (b + b.T) for (a, _), b in zip(parts, cross)]
+                mixer = [split(coef_b * a + coef_c * b) for a, b in zip(gram, square)]
+                low = [(a - b.astype(F32)).astype(BF) for a, b in zip(cur, high)]
+                change = [nn(a, b) + (nn(a, d) + nn(e, b)) for a, e, (b, d) in zip(high, low, mixer)]
+            cur = [coef_a * a + b for a, b in zip(cur, change)]
         step = step_ref[c]
         for m in range(3):
-            new = w[m] - step * xs[m]
+            new = w[m] - step * cur[m]
             w[m] = new
             wb[m] = new.astype(BF)
 
@@ -310,15 +314,15 @@
             nn(cb[s, 0, part(j)], wo[group, 0:DH, :]) + nn(cb[s, 1, part(j)], wo[group, DH : 2 * DH, :])
         ).astype(BF)
 
-    def apply(s):
+    def apply(s, send):
         for j in range(2):
             cs[s, part(j)] = fast(s, oc, j)
             cs_copy(s, j).start()
-        for j in range(2):
             cb[s, c, part(j)] = fast(s, c, j)
             cs_copy(s, j).wait_recv()
             zs[s, part(j)] = project(s, j, 1 - hg)
-            z_copy(s, j).start()
+            if send:
+                z_copy(s, j).start()
         for j in range(2):
             cs_copy(s, j).wait_send()
             zo[s, part(j)] = project(s, j, hg)
@@ -332,38 +336,39 @@
             mx[s, part(j)] = (zo[s, part(j)].astype(F32) + zr[s, part(j)].astype(F32)).astype(BF)
         out_copy(s).start()
 
-    local_in(0, 0).wait()
-    local_in(1, 0).wait()
-    forward(0, c, 0)
+    def halo(i, s):
+        buf = (kb, vb)[i]
+        return remote(
+            buf.at[s, pl.ds(TC, WIN)], buf.at[s, pl.ds(0, WIN)], halo_s.at[i, s], halo_r.at[i, s], next_chip
+        )
+
     pl.semaphore_wait(barrier, len(senders))
     to_sibling(0, 0).start()
     to_sibling(1, 0).start()
     rate_copy.start()
     for i, s in ((0, 1), (1, 1), (2, 0), (2, 1)):
         to_sibling(i, s).start()
+    w_copies[2].wait()
+    w[2] = wdb[...].T
+    wb[2] = w[2].astype(BF)
+    local_in(0, 0).wait()
+    local_in(1, 0).wait()
+    forward(0, c, 0)
     forward(0, c, 1)
     to_sibling(0, 0).wait()
     to_sibling(1, 0).wait()
     rate_copy.wait()
+    halo(0, 0).start()
+    halo(1, 0).start()
     forward(0, oc, 0)
     forward(0, oc, 1)
     gradients(0)
 
-    def halo(i, s):
-        buf = (kb, vb)[i]
-        return remote(
-            buf.at[s, pl.ds(TC, WIN)], buf.at[s, pl.ds(0, WIN)], halo_s.at[i, s], halo_r.at[i, s], next_chip
-        )
-
-    halo(0, 0).start()
-    halo(1, 0).start()
     for i in range(3):
         local_in(i, 1).wait()
         to_sibling(i, 1).wait()
     local_in(2, 0).wait()
     to_sibling(2, 0).wait()
-    halo(0, 1).start()
-    halo(1, 1).start()
     for i in range(2):
         wo_copies[i].wait()
 
@@ -372,21 +377,27 @@
     halo(1, 0).wait()
     attend(0, 0, 4)
     spread(0)
-    halo(0, 1).wait()
-    halo(1, 1).wait()
-    attend(1, 0, 4)
+    attend(1, 1, 4)
+    arrive(0)
+    halo(0, 1).start()
+    halo(1, 1).start()
     update(0)
 
     for j in range(2):
         forward(1, c, j)
         forward(1, oc, j)
     gradients(1)
-    apply(0)
+    apply(0, False)
     reduce(1)
+    halo(0, 1).wait()
+    halo(1, 1).wait()
+    attend(1, 0, 1)
     spread(1)
-    finish(0)
+    for j in range(2):
+        z_copy(0, j).start()
+    arrive(1)
     update(1)
-    apply(1)
+    apply(1, True)
 
     outs = (gate_ref.at[c], up_ref.at[c], down_ref.at[c])
     wdb[...] = w[2].T
@@ -394,6 +405,7 @@
     for m in range(3):
         remote(sources[m], outs[m], st_s.at[m], st_r.at[m], sibling).start()
         pltpu.make_async_copy(sources[m], outs[m], w_sem.at[m]).start()
+    finish(0)
     finish(1)
     for m in range(3):
         remote(sources[m], outs[m], st_s.at[m], st_r.at[m], sibling).wait()
@@ -402,6 +414,22 @@
         out_copy(s).wait()
 
 
+def deliver(*refs):
+    ins, outs, bufs, get_sem, put_sem = refs[0:4], refs[4:8], refs[8:12], refs[12], refs[13]
+    gets, puts = [], []
+    for i in (1, 2, 3, 0):
+        for h in range(2):
+            gets.append(pltpu.make_async_copy(ins[i].at[h], bufs[i].at[h], get_sem.at[i, h]))
+            puts.append(pltpu.make_async_copy(bufs[i].at[h], outs[i].at[h], put_sem.at[i, h]))
+    for get in gets:
+        get.start()
+    for get, put in zip(gets, puts):
+        get.wait()
+        put.start()
+    for put in puts:
+        put.wait()
+
+
 def body(queries, keys, values, token_rate, step_size, w_gate, w_up, w_down, w_out):
     dma = pltpu.SemaphoreType.DMA
     anywhere = pl.BlockSpec(memory_space=pl.ANY)
@@ -412,7 +440,7 @@
     def f32(*shape):
         return pltpu.VMEM(shape, F32)
 
-    return pl.pallas_call(
+    results = pl.pallas_call(
         kernel,
         out_shape=(
             jax.ShapeDtypeStruct((SEG, T, 2 * DH), BF),
@@ -422,22 +450,22 @@
         ),
         in_specs=[
             anywhere, anywhere, anywhere,
-            pl.BlockSpec(memory_space=pltpu.VMEM),
+            anywhere,
             pl.BlockSpec(memory_space=pltpu.SMEM),
             anywhere, anywhere, anywhere, anywhere,
         ],
         out_specs=(anywhere, anywhere, anywhere, anywhere),
         scratch_shapes=[
             b16(SEG, TC, DH), b16(SEG, WIN + TC, DH), b16(SEG, WIN + TC, DH),
-            f32(2, 8, T), f32(8, T),
+            f32(2, 8, T), f32(SEG, 2, T), f32(8, T),
             f32(3, FH, DH), b16(3, FH, DH), f32(DH, FH), b16(2, 512, 512),
             b16(FH, TC), b16(FH, TC), b16(FH, TC),
-            f32(3, 8, 64, DH), b16(SEG, 3, 8, 64, DH), b16(SEG, 3, 7, 64, DH), b16(SEG, 3, 4, 64, DH),
-            b16(SEG, 3, 8, 64, DH), f32(3, FH, DH),
+            f32(3, 16, 32, DH), b16(SEG, 3, 16, 32, DH), b16(SEG, 4, 7, 2, 32, DH), b16(SEG, 4, 4, 2, 32, DH),
+            b16(SEG, 3, 16, 32, DH),
             f32(SEG, TC, DH), b16(SEG, T, DH), b16(SEG, 2, T, DH),
             b16(SEG, T, 512), b16(SEG, T, 512), b16(SEG, T, 512), b16(SEG, T, 512),
-            dma((3, 2)), dma((3,)), dma((2,)), dma((3, 2)), dma((3, 2)), dma, dma, dma((2, 2)), dma((2, 2)),
-            dma((2, 3, 7)), dma((2, 3, 7)), dma((2, 3, 3)), dma((2, 3, 3)), dma((2, 3, 7)), dma((2, 3, 7)),
+            dma((3, 2)), dma((3,)), dma((2,)), dma, dma((3, 2)), dma((3, 2)), dma, dma, dma((2, 2)), dma((2, 2)),
+            dma((2, 4, 7)), dma((2, 4, 7)), dma((2, 4, 3)), dma((2, 4, 3)), dma((2, 4, 7)), dma((2, 4, 7)),
             dma((2, 2)), dma((2, 2)), dma((2, 2)), dma((2, 2)), dma((3,)), dma((3,)), dma((2,)),
         ],
         compiler_params=pltpu.CompilerParams(
@@ -445,6 +473,15 @@
         ),
         name="layer",
     )(queries, keys, values, token_rate, step_size, w_gate, w_up, w_down, w_out)
+    return pl.pallas_call(
+        deliver,
+        out_shape=tuple(jax.ShapeDtypeStruct(a.shape, a.dtype) for a in results),
+        in_specs=[anywhere] * 4,
+        out_specs=(anywhere,) * 4,
+        scratch_shapes=[pltpu.VMEM(a.shape, a.dtype) for a in results] + [dma((4, 2)), dma((4, 2))],
+        compiler_params=pltpu.CompilerParams(vmem_limit_bytes=16 * 2**20),
+        name="deliver",
+    )(*results)
 
 
 def solution(mesh):

time: 123 us -> 101 us (0.82)
  Pallas kernels: 116 us -> 95.2 us
  local copies, waits for them, and re-layouts: 6.53 us -> 4.89 us
    pallas_call x1, Pallas kernels: 116 us -> 92.7 us  [body(): pl.pallas_call(kernel, out_shape=(jax.ShapeDtypeStruct((SEG, T, 2 * DH),...]
    pallas_call x0 -> x1, Pallas kernels: none -> 2.42 us  [body(): pl.pallas_call(deliver, out_shape=tuple((jax.ShapeDtypeStruct(a.shape, a....]
    unnamed x10 -> x8, local copies, waits for them, and re-layouts: 6.53 us -> 4.89 us
where the time goes in v2:
time: 101 us
  Pallas kernels  95.2 us (94%)
  local copies, waits for them, and re-layouts  4.89 us (5%)
    pallas_call x1, Pallas kernels, body(): pl.pallas_call(kernel, out_shape=(jax.ShapeDtypeStruct((SEG, T, 2 * DH),...  92.7 us
    unnamed x8, local copies, waits for them, and re-layouts  4.89 us
    pallas_call x1, Pallas kernels, body(): pl.pallas_call(deliver, out_shape=tuple((jax.ShapeDtypeStruct(a.shape, a....  2.42 us

profile of v2, /device:TPU:1, one launch (start us, length us, event | category | flops | bytes accessed | tf_op | source)
XLA Modules:
  0.0 100.9 jit_solution(2497953630317501976)
XLA Ops:
  0.6 92.7 %layer.1 = (bf16[2,512,512]{2,1,0:T(8,128)(2,1)}, f32[2,512,256]{2,1,0:T(8,128)}, f32[2,512,256]{2,1,0:T(8,128)}, f32[2,256,512]{2,1,0:T(8,128)}) custom-call(bf16[2,512,512]{2,1,0:T(8,128)(2,1)} %q_ref.1, bf16[2,512,512]{2,1,0:T(8,128)(2,1)} %k_ref.1, bf16[2,512,512]{2,1,0:T(8,128)(2,1)} %v_ref.1, f32[2,2,512]{2,1,0:T(2,128)} %rate_ref.1, f32[2]{0:T(128)} %step_ref.1, ...), custom_call_target="tpu_custom_call" | custom-call | tf_op jit(solution)/shard_map/layer/pallas_call | solution.py:443
  93.4 0.0 copy-start
  93.4 1.2 %copy-done = bf16[2,512,512]{2,1,0:T(8,128)(2,1)S(1)} copy-done((bf16[2,512,512]{2,1,0:T(8,128)(2,1)S(1)}, bf16[2,512,512]{2,1,0:T(8,128)(2,1)}, u32[]{:S(2)}) %copy-start) | copy-done | bytes 1048600
  94.6 0.0 copy-start.1
  94.6 1.2 %copy-done.1 = f32[2,512,256]{2,1,0:T(8,128)S(1)} copy-done((f32[2,512,256]{2,1,0:T(8,128)S(1)}, f32[2,512,256]{2,1,0:T(8,128)}, u32[]{:S(2)}) %copy-start.1) | copy-done | bytes 1048600
  95.8 0.0 copy-start.2
  95.8 1.2 %copy-done.2 = f32[2,512,256]{2,1,0:T(8,128)S(1)} copy-done((f32[2,512,256]{2,1,0:T(8,128)S(1)}, f32[2,512,256]{2,1,0:T(8,128)}, u32[]{:S(2)}) %copy-start.2) | copy-done | bytes 1048600
  97.0 0.0 copy-start.3
  97.1 1.2 %copy-done.3 = f32[2,256,512]{2,1,0:T(8,128)S(1)} copy-done((f32[2,256,512]{2,1,0:T(8,128)S(1)}, f32[2,256,512]{2,1,0:T(8,128)}, u32[]{:S(2)}) %copy-start.3) | copy-done | bytes 1048600
  98.3 2.4 %deliver.1 = (bf16[2,512,512]{2,1,0:T(8,128)(2,1)}, f32[2,512,256]{2,1,0:T(8,128)}, f32[2,512,256]{2,1,0:T(8,128)}, f32[2,256,512]{2,1,0:T(8,128)}) custom-call(bf16[2,512,512]{2,1,0:T(8,128)(2,1)S(1)} %copy-done, f32[2,512,256]{2,1,0:T(8,128)S(1)} %copy-done.1, f32[2,512,256]{2,1,0:T(8,128)S(1)} %copy-done.2, f32[2,256,512]{2,1,0:T(8,128)S(1)} %copy-done.3), custom_call_target="tpu_custom_call" | custom-call | tf_op jit(solution)/shard_map/deliver/pallas_call | solution.py:476
Async XLA Ops:
  93.4 1.2 %copy-start = (bf16[2,512,512]{2,1,0:T(8,128)(2,1)S(1)}, bf16[2,512,512]{2,1,0:T(8,128)(2,1)}, u32[]{:S(2)}) copy-start(bf16[2,512,512]{2,1,0:T(8,128)(2,1)} %get-tuple-element.8.refs_0_) | copy-start | bytes 3145732
  94.6 1.2 %copy-start.1 = (f32[2,512,256]{2,1,0:T(8,128)S(1)}, f32[2,512,256]{2,1,0:T(8,128)}, u32[]{:S(2)}) copy-start(f32[2,512,256]{2,1,0:T(8,128)} %get-tuple-element.9.refs_1_) | copy-start | bytes 3145732
  95.8 1.2 %copy-start.2 = (f32[2,512,256]{2,1,0:T(8,128)S(1)}, f32[2,512,256]{2,1,0:T(8,128)}, u32[]{:S(2)}) copy-start(f32[2,512,256]{2,1,0:T(8,128)} %get-tuple-element.10.refs_2_) | copy-start | bytes 3145732
  97.0 1.2 %copy-start.3 = (f32[2,256,512]{2,1,0:T(8,128)S(1)}, f32[2,256,512]{2,1,0:T(8,128)}, u32[]{:S(2)}) copy-start(f32[2,256,512]{2,1,0:T(8,128)} %get-tuple-element.11.refs_3_) | copy-start | bytes 3145732

commit v3 on v2

--- a/solution.py
+++ b/solution.py
@@ -18,6 +18,7 @@
 TC = 2 * T
 SEG = 2
 BLK = 256
+ROWS = (256, 128)
 coef_a = 3.4445
 coef_b = -4.775
 coef_c = 2.0315
@@ -292,49 +293,54 @@
 
         lax.fori_loop(first, last, one, 0)
 
-    def fast(s, half, j):
-        start = pl.multiple_of(half * T + j * BLK, BLK)
-        query = qb[s, pl.ds(start, BLK), :]
+    def fast(s, half, rows):
+        start = pl.multiple_of(half * T + rows.start, rows.size)
+        query = qb[s, pl.ds(start, rows.size), :]
         g1 = nt(query, wb[0])
         g3 = nt(query, wb[1])
         hidden = (g1 * sigmoid(g1) * g3).astype(BF)
-        return (att[s, pl.ds(start, BLK), :] + nn(hidden, wb[2])).astype(BF)
-
-    def part(j):
-        return pl.ds(j * BLK, BLK)
+        return (att[s, pl.ds(start, rows.size), :] + nn(hidden, wb[2])).astype(BF)
+
+    def part(s, j):
+        return pl.ds(j * ROWS[s], ROWS[s])
 
     def cs_copy(s, j):
-        return remote(cs.at[s, part(j)], cb.at[s, c, part(j)], cs_s.at[s, j], cs_r.at[s, j], sibling)
+        rows = part(s, j)
+        return remote(cs.at[s, rows], cb.at[s, c, rows], cs_s.at[s, j], cs_r.at[s, j], sibling)
 
     def z_copy(s, j):
-        return remote(zs.at[s, part(j)], zr.at[s, part(j)], zs_s.at[s, j], zs_r.at[s, j], across)
+        rows = part(s, j)
+        return remote(zs.at[s, rows], zr.at[s, rows], zs_s.at[s, j], zs_r.at[s, j], across)
 
     def project(s, j, group):
+        rows = part(s, j)
         return (
-            nn(cb[s, 0, part(j)], wo[group, 0:DH, :]) + nn(cb[s, 1, part(j)], wo[group, DH : 2 * DH, :])
+            nn(cb[s, 0, rows], wo[group, 0:DH, :]) + nn(cb[s, 1, rows], wo[group, DH : 2 * DH, :])
         ).astype(BF)
 
-    def apply(s, send):
-        for j in range(2):
-            cs[s, part(j)] = fast(s, oc, j)
+    def apply(s):
+        count = T // ROWS[s]
+        for j in range(count):
+            cs[s, part(s, j)] = fast(s, oc, part(s, j))
             cs_copy(s, j).start()
-            cb[s, c, part(j)] = fast(s, c, j)
+            cb[s, c, part(s, j)] = fast(s, c, part(s, j))
             cs_copy(s, j).wait_recv()
-            zs[s, part(j)] = project(s, j, 1 - hg)
-            if send:
-                z_copy(s, j).start()
-        for j in range(2):
+            zs[s, part(s, j)] = project(s, j, 1 - hg)
+            z_copy(s, j).start()
+        for j in range(count):
             cs_copy(s, j).wait_send()
-            zo[s, part(j)] = project(s, j, hg)
-
-    def out_copy(s):
-        return pltpu.make_async_copy(mx.at[s], mixed_ref.at[s], out_sem.at[s])
+            zo[s, part(s, j)] = project(s, j, hg)
+
+    def out_copy(s, j):
+        rows = part(s, j)
+        return pltpu.make_async_copy(mx.at[s, rows], mixed_ref.at[s, rows], out_sem.at[s, j])
 
     def finish(s):
-        for j in range(2):
+        for j in range(T // ROWS[s]):
+            rows = part(s, j)
             z_copy(s, j).wait()
-            mx[s, part(j)] = (zo[s, part(j)].astype(F32) + zr[s, part(j)].astype(F32)).astype(BF)
-        out_copy(s).start()
+            mx[s, rows] = (zo[s, rows].astype(F32) + zr[s, rows].astype(F32)).astype(BF)
+            out_copy(s, j).start()
 
     def halo(i, s):
         buf = (kb, vb)[i]
@@ -358,8 +364,6 @@
     to_sibling(0, 0).wait()
     to_sibling(1, 0).wait()
     rate_copy.wait()
-    halo(0, 0).start()
-    halo(1, 0).start()
     forward(0, oc, 0)
     forward(0, oc, 1)
     gradients(0)
@@ -373,31 +377,29 @@
         wo_copies[i].wait()
 
     reduce(0)
-    halo(0, 0).wait()
-    halo(1, 0).wait()
-    attend(0, 0, 4)
+    attend(0, 1, 4)
     spread(0)
-    attend(1, 1, 4)
     arrive(0)
-    halo(0, 1).start()
-    halo(1, 1).start()
+    halos = [halo(i, s) for s in range(SEG) for i in range(2)]
+    for copy in halos:
+        copy.start()
     update(0)
 
     for j in range(2):
         forward(1, c, j)
         forward(1, oc, j)
     gradients(1)
-    apply(0, False)
+    attend(1, 1, 4)
     reduce(1)
-    halo(0, 1).wait()
-    halo(1, 1).wait()
+    for copy in halos:
+        copy.wait()
+    attend(0, 0, 1)
     attend(1, 0, 1)
     spread(1)
-    for j in range(2):
-        z_copy(0, j).start()
+    apply(0)
     arrive(1)
     update(1)
-    apply(1, True)
+    apply(1)
 
     outs = (gate_ref.at[c], up_ref.at[c], down_ref.at[c])
     wdb[...] = w[2].T
@@ -411,7 +413,8 @@
         remote(sources[m], outs[m], st_s.at[m], st_r.at[m], sibling).wait()
         pltpu.make_async_copy(sources[m], outs[m], w_sem.at[m]).wait()
     for s in range(SEG):
-        out_copy(s).wait()
+        for j in range(T // ROWS[s]):
+            out_copy(s, j).wait()
 
 
 def deliver(*refs):
@@ -466,7 +469,7 @@
             b16(SEG, T, 512), b16(SEG, T, 512), b16(SEG, T, 512), b16(SEG, T, 512),
             dma((3, 2)), dma((3,)), dma((2,)), dma, dma((3, 2)), dma((3, 2)), dma, dma, dma((2, 2)), dma((2, 2)),
             dma((2, 4, 7)), dma((2, 4, 7)), dma((2, 4, 3)), dma((2, 4, 3)), dma((2, 4, 7)), dma((2, 4, 7)),
-            dma((2, 2)), dma((2, 2)), dma((2, 2)), dma((2, 2)), dma((3,)), dma((3,)), dma((2,)),
+            dma((2, 4)), dma((2, 4)), dma((2, 4)), dma((2, 4)), dma((3,)), dma((3,)), dma((2, 4)),
         ],
         compiler_params=pltpu.CompilerParams(
             collective_id=0, has_side_effects=True, vmem_limit_bytes=56 * 2**20
@@ -479,7 +482,7 @@
         in_specs=[anywhere] * 4,
         out_specs=(anywhere,) * 4,
         scratch_shapes=[pltpu.VMEM(a.shape, a.dtype) for a in results] + [dma((4, 2)), dma((4, 2))],
-        compiler_params=pltpu.CompilerParams(vmem_limit_bytes=16 * 2**20),
+        compiler_params=pltpu.CompilerParams(vmem_limit_bytes=60 * 2**20),
         name="deliver",
     )(*results)
 

time: 101 us -> 95.2 us (0.943)
  local copies, waits for them, and re-layouts: 4.89 us -> 0 us
    unnamed x8 -> x0, local copies, waits for them, and re-layouts: 4.89 us -> none
    pallas_call x1, Pallas kernels: 92.7 us -> 90.6 us  [body(): pl.pallas_call(kernel, out_shape=(jax.ShapeDtypeStruct((SEG, T, 2 * DH),...]
    pallas_call x1, Pallas kernels: 2.42 us -> 3.58 us  [body(): pl.pallas_call(deliver, out_shape=tuple((jax.ShapeDtypeStruct(a.shape, a....]
where the time goes in v3:
time: 95.2 us; the launch traced here: 95 us
  Pallas kernels  94.2 us (99%)
    pallas_call x1, Pallas kernels, body(): pl.pallas_call(kernel, out_shape=(jax.ShapeDtypeStruct((SEG, T, 2 * DH),...  90.6 us
    pallas_call x1, Pallas kernels, body(): pl.pallas_call(deliver, out_shape=tuple((jax.ShapeDtypeStruct(a.shape, a....  3.58 us

profile of v3, /device:TPU:1, one launch (start us, length us, event | category | flops | bytes accessed | tf_op | source)
XLA Modules:
  0.0 95.0 jit_solution(397222453049963447)
XLA Ops:
  0.6 90.6 %layer.1 = (bf16[2,512,512]{2,1,0:T(8,128)(2,1)}, f32[2,512,256]{2,1,0:T(8,128)}, f32[2,512,256]{2,1,0:T(8,128)}, f32[2,256,512]{2,1,0:T(8,128)}) custom-call(bf16[2,512,512]{2,1,0:T(8,128)(2,1)} %q_ref.1, bf16[2,512,512]{2,1,0:T(8,128)(2,1)} %k_ref.1, bf16[2,512,512]{2,1,0:T(8,128)(2,1)} %v_ref.1, f32[2,2,512]{2,1,0:T(2,128)} %rate_ref.1, f32[2]{0:T(128)} %step_ref.1, ...), custom_call_target="tpu_custom_call" | custom-call | tf_op jit(solution)/shard_map/layer/pallas_call | solution.py:446
  91.3 3.6 %deliver.1 = (bf16[2,512,512]{2,1,0:T(8,128)(2,1)}, f32[2,512,256]{2,1,0:T(8,128)}, f32[2,512,256]{2,1,0:T(8,128)}, f32[2,256,512]{2,1,0:T(8,128)}) custom-call(bf16[2,512,512]{2,1,0:T(8,128)(2,1)} %get-tuple-element.8.refs_0_, f32[2,512,256]{2,1,0:T(8,128)} %get-tuple-element.9.refs_1_, f32[2,512,256]{2,1,0:T(8,128)} %get-tuple-element.10.refs_2_, ...), custom_call_target="tpu_custom_call" | custom-call | tf_op jit(solution)/shard_map/deliver/pallas_call | solution.py:479

commit v4 on v3

--- a/solution.py
+++ b/solution.py
@@ -27,7 +27,7 @@
 SINGLE_STEPS = 3
 SPLIT_STEPS = 2
 
-JOBS = ((2, 0, 2, 0, 0), (0, 0, 2, 1, 0), (1, 0, 1, 0, 1), (1, 8, 1, 1, 1))
+JOBS = ((2, 0, 2, 2, 0), (0, 0, 2, 3, 0), (1, 0, 1, 0, 0), (1, 8, 1, 1, 0))
 
 
 def nn(a, b):
@@ -79,6 +79,9 @@
     def group8(job, k):
         _, _, _, line, shift = JOBS[job]
         r, b = k // 2, k % 2
+        if line > 1:
+            along, pz = lax.rem((x if line == 3 else y) + r, 4), lax.rem(z + b, 2)
+            return (at(along, y, pz) if line == 3 else at(x, along, pz)), along * 2 + pz
         along, beside = (x, y) if line else (y, x)
         bit = lax.rem(beside + shift, 2)
         along = lax.rem(along + r, 4)
@@ -88,6 +91,9 @@
 
     def group4(job, k):
         _, _, _, line, shift = JOBS[job]
+        if line > 1:
+            across_line = lax.rem((y if line == 3 else x) + k, 4)
+            return (at(x, across_line, z) if line == 3 else at(across_line, y, z)), across_line
         beside, pz = lax.rem((y if line else x) + 2 * (k // 2), 4), lax.rem(z + k % 2, 2)
         index = (lax.rem(beside + shift, 4) // 2) * 2 + pz
         return (at(x, beside, pz) if line else at(beside, y, pz)), index
@@ -103,7 +109,7 @@
 
     barrier = pltpu.get_barrier_semaphore()
     offsets = [(i, j, 0) for i in range(4) for j in range(4) if (i, j) not in ((0, 0), (2, 2))]
-    offsets += [(0, 0, 1), (0, 2, 1), (2, 0, 1)]
+    offsets += [(0, j, 1) for j in range(4)] + [(i, 0, 1) for i in range(1, 4)]
     senders = [at(lax.rem(x + i, 4), lax.rem(y + j, 4), lax.rem(z + k, 2)) for i, j, k in offsets]
     senders += [sibling, across, prev_chip]
     for device in senders:

time: 95.2 us -> 92.5 us (0.972)
  Pallas kernels: 94.2 us -> 91.5 us
    pallas_call x1, Pallas kernels: 90.6 us -> 88 us  [body(): pl.pallas_call(kernel, out_shape=(jax.ShapeDtypeStruct((SEG, T, 2 * DH),...]
where the time goes in v4:
time: 92.5 us; the launch traced here: 92.4 us
  Pallas kernels  91.5 us (99%)
    pallas_call x1, Pallas kernels, body(): pl.pallas_call(kernel, out_shape=(jax.ShapeDtypeStruct((SEG, T, 2 * DH),...  88 us
    pallas_call x1, Pallas kernels, body(): pl.pallas_call(deliver, out_shape=tuple((jax.ShapeDtypeStruct(a.shape, a....  3.58 us

profile of v4, /device:TPU:1, one launch (start us, length us, event | category | flops | bytes accessed | tf_op | source)
XLA Modules:
  0.0 92.4 jit_solution(6330716888680617469)
XLA Ops:
  0.6 88.0 %layer.1 = (bf16[2,512,512]{2,1,0:T(8,128)(2,1)}, f32[2,512,256]{2,1,0:T(8,128)}, f32[2,512,256]{2,1,0:T(8,128)}, f32[2,256,512]{2,1,0:T(8,128)}) custom-call(bf16[2,512,512]{2,1,0:T(8,128)(2,1)} %q_ref.1, bf16[2,512,512]{2,1,0:T(8,128)(2,1)} %k_ref.1, bf16[2,512,512]{2,1,0:T(8,128)(2,1)} %v_ref.1, f32[2,2,512]{2,1,0:T(2,128)} %rate_ref.1, f32[2]{0:T(128)} %step_ref.1, ...), custom_call_target="tpu_custom_call" | custom-call | tf_op jit(solution)/shard_map/layer/pallas_call | solution.py:452
  88.6 3.6 %deliver.1 = (bf16[2,512,512]{2,1,0:T(8,128)(2,1)}, f32[2,512,256]{2,1,0:T(8,128)}, f32[2,512,256]{2,1,0:T(8,128)}, f32[2,256,512]{2,1,0:T(8,128)}) custom-call(bf16[2,512,512]{2,1,0:T(8,128)(2,1)} %get-tuple-element.8.refs_0_, f32[2,512,256]{2,1,0:T(8,128)} %get-tuple-element.9.refs_1_, f32[2,512,256]{2,1,0:T(8,128)} %get-tuple-element.10.refs_2_, ...), custom_call_target="tpu_custom_call" | custom-call | tf_op jit(solution)/shard_map/deliver/pallas_call | solution.py:485
